TPU v7x, 32 devices: a whole 2x2x4 slice. The times are simulated.
32 devices in a mesh: group: 2 (over y), blk: 4 (over x, core), rep: 4 (over z).
Axes of the slice: x: 2, y: 2, z: 4, core: 2. Of those that a mesh axis runs over, the one named last changes fastest.
Arguments:
- feats: bfloat16 [12288, 128], P(('group', 'blk')), parts along dimension 0, may hold values from -6 to 6
- tiles: bfloat16 [96, 24, 128, 128], P(('group', 'blk'), None, 'rep'), parts along dimension 0, may hold values from -0.109375 to 0.109375
- col_local: int32 [96, 24], P(('group', 'blk')), parts along dimension 0, may hold values from 0 to 11, as said below
- tile_count: int32 [96, 4], P(('group', 'blk')), parts along dimension 0, may hold values from 0 to 6, as said below
- w_self: bfloat16 [2, 128, 128], replicated, may hold values from -0.5 to 0.5
- w_neigh: bfloat16 [2, 128, 128], replicated, may hold values from -0.5 to 0.5
- bias: float32 [2, 128], replicated, may hold values from -3 to 3
- cotangent: bfloat16 [12288, 128], P(('group', 'blk')), parts along dimension 0, may hold values from -0.076171875 to 0.076171875
Outputs:
- logits: bfloat16 [12288, 128], P(('group', 'blk')), parts along dimension 0
- grad_self: float32 [4, 128, 128], P('group'), parts along dimension 0
- grad_neigh: float32 [4, 128, 128], P('group'), parts along dimension 0
- grad_bias: float32 [4, 128], P('group'), parts along dimension 0
There are 2 independent parts, one for each index of `group`. A program takes and returns all parts, laid end to end along the dimension named above; an argument that names none is the same for every part. Nothing has to cross between parts.
Inputs may be any that keep to these rules, and one draw needn't show every extreme that they name: `col_local`: the column block of a slot is one of the 12 row blocks held by that slot's source index of blk; the 6 slots of one row block and one source name distinct column blocks. The live tiles are the first tile_count slots of each group of 6; some entry equals 6.
All inputs are finite; a program needn't handle non-finite values.
Results may differ from a plain program's by a relative error of at most 0.0062.
Values may be sent and summed in bfloat16 or wider, within the bound.
A program may use at most 64 MiB of HBM per device.

v0:
```python
import jax
import jax.numpy as jnp
from jax import lax
from jax.sharding import PartitionSpec as P


def from_behind(block, axis, distance):
    devices = range(lax.axis_size(axis))
    route = [((i - distance) % len(devices), i) for i in devices]
    return lax.ppermute(block, axis, route)


def shards(feats, tiles, col_local, tile_count, w_self, w_neigh, bias, cotangent):
    cycle_size = lax.axis_size("blk")
    my_index = lax.axis_index("blk")
    rep_index = lax.axis_index("rep")
    row_blocks = tiles.shape[0]
    slot_count = tiles.shape[1] // cycle_size
    share = tiles.shape[2]
    tile_edge = tiles.shape[3]
    width = feats.shape[1]
    zeros = jnp.zeros((row_blocks, tile_edge, width), jnp.float32)
    share_zeros = jnp.zeros((row_blocks, share, width), jnp.float32)

    def my_share_rows(rows):
        blocks = rows.reshape(row_blocks, tile_edge, width)
        return lax.dynamic_slice_in_dim(blocks, rep_index * share, share, 1)

    def selector_for(source):
        columns = lax.dynamic_slice_in_dim(col_local, source * slot_count, slot_count, 1)
        counts = lax.dynamic_slice_in_dim(tile_count, source, 1, 1)
        alive_mask = jnp.arange(slot_count, dtype=jnp.int32)[None, :] < counts
        chosen = (
            columns[:, :, None] == jnp.arange(row_blocks, dtype=jnp.int32)[None, None, :]
        ) & alive_mask[:, :, None]
        tile_group = lax.dynamic_slice_in_dim(tiles, source * slot_count, slot_count, 1)
        return (tile_group, chosen)

    def source_term(visiting, source):
        tile_group, chosen = selector_for(source)
        picked = jnp.einsum(
            "rkc,cjf->rkjf",
            chosen.astype(jnp.bfloat16),
            visiting,
            preferred_element_type=jnp.float32,
        ).astype(jnp.bfloat16)
        return jnp.einsum("rkji,rkjf->rif", tile_group, picked, preferred_element_type=jnp.float32)

    def target_term(grad_blocks, target):
        tile_group, chosen = selector_for(target)
        product = jnp.einsum(
            "rkji,rif->rkjf", tile_group, grad_blocks, preferred_element_type=jnp.float32
        )
        return jnp.einsum(
            "rkc,rkjf->cjf", chosen.astype(jnp.float32), product, precision=lax.Precision.HIGHEST
        )

    def over_rep(partial_value):
        my_part = lax.psum_scatter(partial_value, "rep", scatter_dimension=0, tiled=True)
        result = lax.all_gather(my_part.astype(jnp.bfloat16), "rep", axis=0, tiled=True)
        return result

    def aggregate(hidden):
        own_share = my_share_rows(hidden)

        def aggregate_cycle_turn(turn, carried):
            running, visiting = carried
            source = (my_index - turn) % cycle_size
            running = running + source_term(visiting, source)
            return (running, from_behind(visiting, "blk", 1))

        running, visiting = lax.fori_loop(
            0, cycle_size - 1, aggregate_cycle_turn, (zeros, own_share)
        )
        running = running + source_term(visiting, (my_index - cycle_size + 1) % cycle_size)
        return over_rep(running.reshape(hidden.shape))

    agg0 = aggregate(feats)
    z0 = (
        jnp.dot(feats, w_self[0], preferred_element_type=jnp.float32)
        + jnp.dot(agg0, w_neigh[0], preferred_element_type=jnp.float32)
        + bias[0]
    )
    h1 = jax.nn.silu(z0).astype(jnp.bfloat16)
    agg1 = aggregate(h1)
    z1 = (
        jnp.dot(h1, w_self[1], preferred_element_type=jnp.float32)
        + jnp.dot(agg1, w_neigh[1], preferred_element_type=jnp.float32)
        + bias[1]
    )
    logits = z1.astype(jnp.bfloat16)
    linear_part = jnp.dot(cotangent, w_self[1].T, preferred_element_type=jnp.float32)
    back1 = jnp.dot(cotangent, w_neigh[1].T, preferred_element_type=jnp.float32).astype(
        jnp.bfloat16
    )
    grad_blocks = back1.reshape(row_blocks, tile_edge, width)

    def spread_cycle_turn(turn, running):
        target = (my_index - 1 - turn) % cycle_size
        return from_behind(running + target_term(grad_blocks, target), "blk", 1)

    running = lax.fori_loop(0, cycle_size - 1, spread_cycle_turn, share_zeros)
    running = running + target_term(grad_blocks, my_index)
    dh_share = (my_share_rows(linear_part) + running).astype(jnp.bfloat16)
    dh1 = lax.all_gather(dh_share, "rep", axis=1, tiled=True).reshape(feats.shape)
    sigma = jax.nn.sigmoid(z0)
    dz0 = (dh1.astype(jnp.float32) * sigma * (1.0 + z0 * (1.0 - sigma))).astype(jnp.bfloat16)
    self_zero = jnp.einsum("nf,ng->fg", feats, dz0, preferred_element_type=jnp.float32)
    self_one = jnp.einsum("nf,ng->fg", h1, cotangent, preferred_element_type=jnp.float32)
    neigh_zero = jnp.einsum("nf,ng->fg", agg0, dz0, preferred_element_type=jnp.float32)
    neigh_one = jnp.einsum("nf,ng->fg", agg1, cotangent, preferred_element_type=jnp.float32)
    bias_zero = jnp.sum(dz0.astype(jnp.float32), axis=0)
    bias_one = jnp.sum(cotangent.astype(jnp.float32), axis=0)
    grad_self, grad_neigh, grad_bias = lax.psum(
        (
            jnp.stack([self_zero, self_one]),
            jnp.stack([neigh_zero, neigh_one]),
            jnp.stack([bias_zero, bias_one]),
        ),
        "blk",
    )
    return (logits, grad_self, grad_neigh, grad_bias)


def solution(mesh):
    return jax.shard_map(
        shards,
        mesh=mesh,
        in_specs=(
            P(("group", "blk"), None),
            P(("group", "blk"), None, "rep", None),
            P(("group", "blk"), None),
            P(("group", "blk"), None),
            P(),
            P(),
            P(),
            P(("group", "blk"), None),
        ),
        out_specs=(
            P(("group", "blk"), None),
            P("group", None, None),
            P("group", None, None),
            P("group", None),
        ),
        check_vma=False,
    )
```

profile of v0, /device:TPU:1, one launch (start us, length us, event | category | flops | bytes accessed | tf_op | source)
XLA Modules:
  0.0 215.5 jit_solution(2466326938847198302)
XLA Ops:
  9.5 14.4 %while.52 = (s32[]{:T(128)}, f32[12,128,128]{2,1,0:T(8,128)S(1)}, bf16[12,32,128]{2,1,0:T(8,128)(2,1)S(1)}, s32[]{:T(128)}, bf16[12,24,32,128]{3,2,1,0:T(8,128)(...) while((s32[]{:T(128)}, f32[12,128,128]{2,1,0:T(8,128)S(1)}, ...), condition=%wide.region_1.2_spmd.clone, body=%wide.region_0.1_spmd.clone.sunk | while | flops 82970400 | bytes 4032004 | solution.py:72
  9.5 2.7 %collective-permute-start.1 = (bf16[12,32,128]{2,1,0:T(8,128)(2,1)S(1)}, bf16[12,32,128]{2,1,0:T(8,128)(2,1)S(1)}, u32[]{:S(2)}, u32[]{:S(2)}) collective-permute-start(bf16[12,32,128]{2,1,0:T(8,128)(2,1)S(1)} %copy.93), channel_id=1, source_target_pairs={{12,0},{0,4},{4,8},{8,12},{13,1},{1,5},{5,9},{9,13},{14,2},{2,6},{... | collective-permute-start | bytes 294920 | tf_op jit(solution)/shard_map/while/body/eval_jaxpr/ppermute | solution.py:10
  14.1 1.6 fusion.142
  18.2 1.6 fusion.142
  22.3 1.6 fusion.142
  24.4 2.5 %fusion.45 = f32[12,128,128]{2,1,0:T(8,128)} fusion(f32[12,128,128]{2,1,0:T(8,128)S(1)} %get-tuple-element.540, bf16[12,6,32,128]{3,1,2,0:T(8,128)(2,1)S(1)} %fusion.60, bf16[12,24,32,128]{3,2,1,0:T(8,128)(2,1)} %get-tuple-element.913, s32[]{:T(128)S(6)} %select_n.147), kind=kOutput, calls=%fused_computation.59 | convolution fusion | flops 75694080 | bytes 2752516 | tf_op jit(solution)/shard_map/rkji,rkjf->rif/dot_general | solution.py:47
  32.4 2.2 %fusion.69 = f32[12,128,128]{2,1,0:T(8,128)} fusion(bf16[12,128,128]{2,1,0:T(8,128)(2,1)} %bitcast.161, bf16[2,128,128]{2,1,0:T(8,128)(2,1)} %param.18), kind=kOutput, calls=%fused_computation.94 | convolution fusion | flops 50331648 | bytes 1212416 | tf_op jit(solution)/shard_map/dot_general | solution.py:92
  34.5 3.4 %fusion.47 = f32[12,32,128]{2,0,1:T(8,128)} fusion(f32[12,6,32,128]{3,2,1,0:T(8,128)} %fusion.52, s32[12,6]{0,1:T(8,128)S(1)} %copy-done.15, pred[12,6]{0,1:T(8,128)(4,1)S(1)} %iota_compare_fusion.9), kind=kOutput, calls=%fused_computation.63 | convolution fusion | flops 42469056 | bytes 1376616 | tf_op jit(solution)/shard_map/rkc,rkjf->cjf/dot_general | solution.py:54
  38.6 33.8 %while.51 = (s32[]{:T(128)}, f32[12,32,128]{2,0,1:T(8,128)}, s32[]{:T(128)}, s32[12,24]{0,1:T(8,128)}, s32[12,4]{0,1:T(4,128)}, /*index=5*/bf16[12,24,32,128]{3,...) while((s32[]{:T(128)}, f32[12,32,128]{2,0,1:T(8,128)}, ...), condition=%wide.region_7.8_spmd, body=%wide.region_6.7_spmd.sunk | while | flops 118015768 | bytes 4523514 | solution.py:102
  41.4 3.1 %fusion.136 = f32[12,32,128]{2,0,1:T(8,128)} fusion(f32[12,32,128]{2,0,1:T(8,128)} %get-tuple-element.800, f32[12,6,32,128]{3,2,1,0:T(8,128)S(1)} %fusion.134, s32[12,6]{0,1:T(8,128)S(1)} %constant_dynamic-slice_fusion.15, pred[12,6]{0,1:T(8,128)(4,1)S(1)} %iota_compare_fusion.13), kind=kOutput, calls=%fused_computation.3.clone.1 | convolution fusion | flops 42518208 | bytes 1573224 | tf_op jit(solution)/shard_map/while/body/eval_jaxpr/rkc,rkjf->cjf/dot_general | solution.py:54
  44.9 3.6 %collective-permute-done = f32[12,32,128]{2,0,1:T(8,128)} collective-permute-done((f32[12,32,128]{2,0,1:T(8,128)}, f32[12,32,128]{2,0,1:T(8,128)}, u32[]{:S(2)}, u32[]{:S(2)}) %collective-permute-start) | collective-permute-done | bytes 196640 | tf_op jit(solution)/shard_map/while/body/eval_jaxpr/ppermute | solution.py:10
  51.3 3.1 %fusion.136 = f32[12,32,128]{2,0,1:T(8,128)} fusion(f32[12,32,128]{2,0,1:T(8,128)} %get-tuple-element.800, f32[12,6,32,128]{3,2,1,0:T(8,128)S(1)} %fusion.134, s32[12,6]{0,1:T(8,128)S(1)} %constant_dynamic-slice_fusion.15, pred[12,6]{0,1:T(8,128)(4,1)S(1)} %iota_compare_fusion.13), kind=kOutput, calls=%fused_computation.3.clone.1 | convolution fusion | flops 42518208 | bytes 1573224 | tf_op jit(solution)/shard_map/while/body/eval_jaxpr/rkc,rkjf->cjf/dot_general | solution.py:54
  54.4 2.5 %collective-permute-start = (f32[12,32,128]{2,0,1:T(8,128)}, f32[12,32,128]{2,0,1:T(8,128)}, u32[]{:S(2)}, u32[]{:S(2)}) collective-permute-start(f32[12,32,128]{2,0,1:T(8,128)} %fusion.136), channel_id=1, source_target_pairs={{12,0},{0,4},{4,8},{8,12},{13,1},{1,5},{5,9},{9,13},{14,2},{2,6},{... | collective-permute-start | bytes 589832 | tf_op jit(solution)/shard_map/while/body/eval_jaxpr/ppermute | solution.py:10
  56.9 3.6 %collective-permute-done = f32[12,32,128]{2,0,1:T(8,128)} collective-permute-done((f32[12,32,128]{2,0,1:T(8,128)}, f32[12,32,128]{2,0,1:T(8,128)}, u32[]{:S(2)}, u32[]{:S(2)}) %collective-permute-start) | collective-permute-done | bytes 196640 | tf_op jit(solution)/shard_map/while/body/eval_jaxpr/ppermute | solution.py:10
  63.2 3.1 %fusion.136 = f32[12,32,128]{2,0,1:T(8,128)} fusion(f32[12,32,128]{2,0,1:T(8,128)} %get-tuple-element.800, f32[12,6,32,128]{3,2,1,0:T(8,128)S(1)} %fusion.134, s32[12,6]{0,1:T(8,128)S(1)} %constant_dynamic-slice_fusion.15, pred[12,6]{0,1:T(8,128)(4,1)S(1)} %iota_compare_fusion.13), kind=kOutput, calls=%fused_computation.3.clone.1 | convolution fusion | flops 42518208 | bytes 1573224 | tf_op jit(solution)/shard_map/while/body/eval_jaxpr/rkc,rkjf->cjf/dot_general | solution.py:54
  66.3 2.5 %collective-permute-start = (f32[12,32,128]{2,0,1:T(8,128)}, f32[12,32,128]{2,0,1:T(8,128)}, u32[]{:S(2)}, u32[]{:S(2)}) collective-permute-start(f32[12,32,128]{2,0,1:T(8,128)} %fusion.136), channel_id=1, source_target_pairs={{12,0},{0,4},{4,8},{8,12},{13,1},{1,5},{5,9},{9,13},{14,2},{2,6},{... | collective-permute-start | bytes 589832 | tf_op jit(solution)/shard_map/while/body/eval_jaxpr/ppermute | solution.py:10
  68.8 3.6 %collective-permute-done = f32[12,32,128]{2,0,1:T(8,128)} collective-permute-done((f32[12,32,128]{2,0,1:T(8,128)}, f32[12,32,128]{2,0,1:T(8,128)}, u32[]{:S(2)}, u32[]{:S(2)}) %collective-permute-start) | collective-permute-done | bytes 196640 | tf_op jit(solution)/shard_map/while/body/eval_jaxpr/ppermute | solution.py:10
  73.6 12.8 %all_gather.11 = bf16[12,128,128]{2,1,0:T(8,128)(2,1)} all-gather(bf16[12,32,128]{2,1,0:T(8,128)(2,1)S(1)} %fusion.57), channel_id=1, replica_groups=mesh['group'=2,'blk'=4,'rep'=4] {'rep'}, dimensions={1}, use_global_device_ids=true | all-gather | bytes 491520 | tf_op jit(solution)/shard_map/all_gather | solution.py:105
  87.0 1.9 fusion.76
  89.8 12.0 %all_gather.9 = bf16[1536,128]{1,0:T(8,128)(2,1)S(1)} all-gather(bf16[384,128]{1,0:T(8,128)(2,1)S(1)} %convert_element_type.72), channel_id=1, replica_groups=mesh['group'=2,'blk'=4,'rep'=4] {'rep'}, dimensions={0}, use_global_device_ids=true | all-gather | bytes 491520 | tf_op jit(solution)/shard_map/all_gather | solution.py:60
  101.9 3.2 %convert_reduce_fusion.1 = (f32[128]{0:T(128)}, bf16[1536,128]{1,0:T(8,128)(2,1)}, bf16[1536,128]{1,0:T(8,128)(2,1)S(1)}) fusion(bf16[12,128,128]{2,1,0:T(8,128)(2,1)} %all_gather.11, f32[128]{0:T(128)S(1)} %get-tuple-element.656, f32[1536,128]{1,0:T(8,128)} %fusion.76, bf16[1536,128]{1,0:T(8,128)(2,1)S(1)} %all_gather.9, bf16[2,128,128]{2,1,0:T(8,128)(2,1)} %param.19), kind=kOutput, calls=%fused_computation.72 | convolution fusion | flops 53477248 | bytes 2393088 | tf_op jit(solution)/shard_map/dot_general | solution.py:81
  106.5 24.3 %while.53 = (s32[]{:T(128)}, f32[12,128,128]{2,1,0:T(8,128)S(1)}, bf16[12,32,128]{2,1,0:T(8,128)(2,1)}, s32[]{:T(128)}, bf16[12,24,32,128]{3,2,1,0:T(8,128)(2,1)...) while((s32[]{:T(128)}, f32[12,128,128]{2,1,0:T(8,128)S(1)}, ...), condition=%wide.region_4.5_spmd.clone, body=%wide.region_3.4_spmd.clone.sunk | while | flops 82970400 | bytes 4228612 | solution.py:72
  108.0 8.3 %collective-permute-start.2 = (bf16[12,32,128]{2,1,0:T(8,128)(2,1)}, bf16[12,32,128]{2,1,0:T(8,128)(2,1)}, u32[]{:S(2)}, u32[]{:S(2)}) collective-permute-start(bf16[12,32,128]{2,1,0:T(8,128)(2,1)} %copy.102), channel_id=1, source_target_pairs={{12,0},{0,4},{4,8},{8,12},{13,1},{1,5},{5,9},{9,13},{14,2},{2,6},{... | collective-permute-start | bytes 294920 | tf_op jit(solution)/shard_map/while/body/eval_jaxpr/ppermute | solution.py:10
  119.0 1.5 copy.102
  120.5 1.7 collective-permute-start.2
  126.4 1.7 collective-permute-start.2
  134.8 6.3 %psum.23 = f32[2,128]{1,0:T(2,128)} all-reduce(f32[2,128]{1,0:T(2,128)S(1)} %pad_maximum_fusion.2), channel_id=1, replica_groups=mesh['group'=2,'blk'=4,'rep'=4] {'blk'}, use_global_device_ids=true, to_apply=%region_12.13 | all-reduce | flops 256 | bytes 2048 | tf_op jit(solution)/shard_map/psum | solution.py:114
  145.2 12.0 %reduce-scatter.5.cloned.1.call-done = f32[384,128]{1,0:T(8,128)} async-done(((f32[1536,128]{1,0:T(8,128)}), f32[384,128]{1,0:T(8,128)}) %reduce-scatter.5.cloned.1.call-update) | async-done | bytes 196624 | tf_op jit(solution)/shard_map/reduce_scatter | solution.py:59
  158.2 12.8 %all_gather.10 = bf16[1536,128]{1,0:T(8,128)(2,1)S(1)} all-gather(bf16[384,128]{1,0:T(8,128)(2,1)S(1)} %convert_element_type.75), channel_id=1, replica_groups=mesh['group'=2,'blk'=4,'rep'=4] {'rep'}, dimensions={0}, use_global_device_ids=true | all-gather | bytes 491520 | tf_op jit(solution)/shard_map/all_gather | solution.py:60
  173.0 32.7 %all-reduce.3.cloned.1.call-done = (f32[2,128,128]{1,2,0:T(8,128)}, f32[2,128,128]{2,1,0:T(8,128)}) async-done(((f32[2,128,128]{1,2,0:T(8,128)}, f32[2,128,128]{2,1,0:T(8,128)}), (f32[2,128,128]{1,2,0:T(8,128)}, f32[2,128,128]{2,1,0:T(8,128)})) %all-reduce.3.cloned.1.call-update) | async-done | bytes 262160 | tf_op jit(solution)/shard_map/psum | solution.py:114
  205.7 1.7 copy.17
  207.4 1.6 copy.108
  (128 shorter events, 50.3 us)
Async XLA Ops:
  7.2 1.5 copy-start
  7.2 81.7 %reduce-scatter.3.cloned.1.call-start = ((), (), s32[]{:S(2)}) async-start(), calls=%async_computation.2 | async-start | bytes 983040 | tf_op jit(solution)/shard_map/reduce_scatter | solution.py:59
  8.6 15.3 %copy-start.13 = (pred[12,6]{1,0:T(8,128)(4,1)}, pred[12,6]{1,0:T(8,128)(4,1)S(1)}, u32[]{:S(2)}) copy-start(pred[12,6]{1,0:T(8,128)(4,1)S(1)} %iota_compare_fusion.8) | copy-start | bytes 220
  9.5 14.5 %copy-start.11 = (s32[12,6]{1,0:T(8,128)}, s32[12,6]{1,0:T(8,128)S(1)}, u32[]{:S(2)}) copy-start(s32[12,6]{1,0:T(8,128)S(1)} %get-tuple-element.652) | copy-start | bytes 868
  9.5 6.2 %collective-permute-start.1 = (bf16[12,32,128]{2,1,0:T(8,128)(2,1)S(1)}, bf16[12,32,128]{2,1,0:T(8,128)(2,1)S(1)}, u32[]{:S(2)}, u32[]{:S(2)}) collective-permute-start(bf16[12,32,128]{2,1,0:T(8,128)(2,1)S(1)} %copy.93), channel_id=1, source_target_pairs={{12,0},{0,4},{4,8},{8,12},{13,1},{1,5},{5,9},{9,13},{14,2},{2,6},{... | collective-permute-start | bytes 294920 | tf_op jit(solution)/shard_map/while/body/eval_jaxpr/ppermute | solution.py:10
  15.7 4.1 %collective-permute-start.1 = (bf16[12,32,128]{2,1,0:T(8,128)(2,1)S(1)}, bf16[12,32,128]{2,1,0:T(8,128)(2,1)S(1)}, u32[]{:S(2)}, u32[]{:S(2)}) collective-permute-start(bf16[12,32,128]{2,1,0:T(8,128)(2,1)S(1)} %copy.93), channel_id=1, source_target_pairs={{12,0},{0,4},{4,8},{8,12},{13,1},{1,5},{5,9},{9,13},{14,2},{2,6},{... | collective-permute-start | bytes 294920 | tf_op jit(solution)/shard_map/while/body/eval_jaxpr/ppermute | solution.py:10
  19.8 4.1 %collective-permute-start.1 = (bf16[12,32,128]{2,1,0:T(8,128)(2,1)S(1)}, bf16[12,32,128]{2,1,0:T(8,128)(2,1)S(1)}, u32[]{:S(2)}, u32[]{:S(2)}) collective-permute-start(bf16[12,32,128]{2,1,0:T(8,128)(2,1)S(1)} %copy.93), channel_id=1, source_target_pairs={{12,0},{0,4},{4,8},{8,12},{13,1},{1,5},{5,9},{9,13},{14,2},{2,6},{... | collective-permute-start | bytes 294920 | tf_op jit(solution)/shard_map/while/body/eval_jaxpr/ppermute | solution.py:10
  23.9 3.0 %copy-start.9 = (s32[12,24]{1,0:T(8,128)S(1)}, s32[12,24]{1,0:T(8,128)}, u32[]{:S(2)}) copy-start(s32[12,24]{1,0:T(8,128)} %get-tuple-element.922) | copy-start | bytes 3460
  24.4 6.6 %copy-start.1 = (bf16[12,24,32,128]{3,2,1,0:T(8,128)(2,1)S(1)}, bf16[12,24,32,128]{3,2,1,0:T(8,128)(2,1)}, u32[]{:S(2)}) copy-start(bf16[12,24,32,128]{3,2,1,0:T(8,128)(2,1)} %get-tuple-element.913) | copy-start | bytes 7077892
  26.9 130.3 %reduce-scatter.5.cloned.1.call-start = ((), (), s32[]{:S(2)}) async-start(), calls=%async_computation.3 | async-start | bytes 983040 | tf_op jit(solution)/shard_map/reduce_scatter | solution.py:59
  28.3 6.2 %copy-start.15 = (s32[12,6]{0,1:T(8,128)S(1)}, s32[12,6]{0,1:T(8,128)}, u32[]{:S(2)}) copy-start(s32[12,6]{0,1:T(8,128)} %copy.13) | copy-start | bytes 868
  30.3 0.7 copy-start.2
  38.6 47.7 %copy-start.17 = (f32[2,128]{1,0:T(2,128)S(1)}, f32[2,128]{1,0:T(2,128)}, u32[]{:S(2)}) copy-start(f32[2,128]{1,0:T(2,128)} %param.20) | copy-start | bytes 3076
  44.4 4.1 %collective-permute-start = (f32[12,32,128]{2,0,1:T(8,128)}, f32[12,32,128]{2,0,1:T(8,128)}, u32[]{:S(2)}, u32[]{:S(2)}) collective-permute-start(f32[12,32,128]{2,0,1:T(8,128)} %fusion.136), channel_id=1, source_target_pairs={{12,0},{0,4},{4,8},{8,12},{13,1},{1,5},{5,9},{9,13},{14,2},{2,6},{... | collective-permute-start | bytes 589832 | tf_op jit(solution)/shard_map/while/body/eval_jaxpr/ppermute | solution.py:10
  54.4 6.1 %collective-permute-start = (f32[12,32,128]{2,0,1:T(8,128)}, f32[12,32,128]{2,0,1:T(8,128)}, u32[]{:S(2)}, u32[]{:S(2)}) collective-permute-start(f32[12,32,128]{2,0,1:T(8,128)} %fusion.136), channel_id=1, source_target_pairs={{12,0},{0,4},{4,8},{8,12},{13,1},{1,5},{5,9},{9,13},{14,2},{2,6},{... | collective-permute-start | bytes 589832 | tf_op jit(solution)/shard_map/while/body/eval_jaxpr/ppermute | solution.py:10
  66.3 6.1 %collective-permute-start = (f32[12,32,128]{2,0,1:T(8,128)}, f32[12,32,128]{2,0,1:T(8,128)}, u32[]{:S(2)}, u32[]{:S(2)}) collective-permute-start(f32[12,32,128]{2,0,1:T(8,128)} %fusion.136), channel_id=1, source_target_pairs={{12,0},{0,4},{4,8},{8,12},{13,1},{1,5},{5,9},{9,13},{14,2},{2,6},{... | collective-permute-start | bytes 589832 | tf_op jit(solution)/shard_map/while/body/eval_jaxpr/ppermute | solution.py:10
  101.9 3.2 %copy-start.6 = (bf16[1536,128]{1,0:T(8,128)(2,1)}, bf16[1536,128]{1,0:T(8,128)(2,1)S(1)}, u32[]{:S(2)}) copy-start(bf16[1536,128]{1,0:T(8,128)(2,1)S(1)} %all_gather.9) | copy-start | bytes 1179652
  105.1 0.7 copy-start.4
  106.5 24.3 %copy-start.14 = (pred[12,6]{1,0:T(8,128)(4,1)S(1)}, pred[12,6]{1,0:T(8,128)(4,1)}, u32[]{:S(2)}) copy-start(pred[12,6]{1,0:T(8,128)(4,1)} %copy-done.13) | copy-start | bytes 220
  108.0 10.9 %collective-permute-start.2 = (bf16[12,32,128]{2,1,0:T(8,128)(2,1)}, bf16[12,32,128]{2,1,0:T(8,128)(2,1)}, u32[]{:S(2)}, u32[]{:S(2)}) collective-permute-start(bf16[12,32,128]{2,1,0:T(8,128)(2,1)} %copy.102), channel_id=1, source_target_pairs={{12,0},{0,4},{4,8},{8,12},{13,1},{1,5},{5,9},{9,13},{14,2},{2,6},{... | collective-permute-start | bytes 294920 | tf_op jit(solution)/shard_map/while/body/eval_jaxpr/ppermute | solution.py:10
  120.5 4.3 %collective-permute-start.2 = (bf16[12,32,128]{2,1,0:T(8,128)(2,1)}, bf16[12,32,128]{2,1,0:T(8,128)(2,1)}, u32[]{:S(2)}, u32[]{:S(2)}) collective-permute-start(bf16[12,32,128]{2,1,0:T(8,128)(2,1)} %copy.102), channel_id=1, source_target_pairs={{12,0},{0,4},{4,8},{8,12},{13,1},{1,5},{5,9},{9,13},{14,2},{2,6},{... | collective-permute-start | bytes 294920 | tf_op jit(solution)/shard_map/while/body/eval_jaxpr/ppermute | solution.py:10
  126.4 4.3 %collective-permute-start.2 = (bf16[12,32,128]{2,1,0:T(8,128)(2,1)}, bf16[12,32,128]{2,1,0:T(8,128)(2,1)}, u32[]{:S(2)}, u32[]{:S(2)}) collective-permute-start(bf16[12,32,128]{2,1,0:T(8,128)(2,1)} %copy.102), channel_id=1, source_target_pairs={{12,0},{0,4},{4,8},{8,12},{13,1},{1,5},{5,9},{9,13},{14,2},{2,6},{... | collective-permute-start | bytes 294920 | tf_op jit(solution)/shard_map/while/body/eval_jaxpr/ppermute | solution.py:10
  130.8 4.0 %copy-start.18 = (f32[128]{0:T(128)S(1)}, f32[128]{0:T(128)}, u32[]{:S(2)}) copy-start(f32[128]{0:T(128)} %get-tuple-element.648) | copy-start | bytes 1540
  133.4 11.2 %copy-start.7 = (bf16[1536,128]{1,0:T(8,128)(2,1)S(1)}, bf16[1536,128]{1,0:T(8,128)(2,1)}, u32[]{:S(2)}) copy-start(bf16[1536,128]{1,0:T(8,128)(2,1)} %copy-done.6) | copy-start | bytes 1179652
  133.4 11.2 %copy-start.8 = (bf16[1536,128]{1,0:T(8,128)(2,1)S(1)}, bf16[1536,128]{1,0:T(8,128)(2,1)}, u32[]{:S(2)}) copy-start(bf16[1536,128]{1,0:T(8,128)(2,1)} %get-tuple-element.649) | copy-start | bytes 1179652
  133.4 11.5 %copy-start.5 = (bf16[1536,128]{1,0:T(8,128)(2,1)S(1)}, bf16[1536,128]{1,0:T(8,128)(2,1)}, u32[]{:S(2)}) copy-start(bf16[1536,128]{1,0:T(8,128)(2,1)} %copy-done.4) | copy-start | bytes 1179652
  133.4 11.6 %copy-start.10 = (bf16[2,128,128]{2,1,0:T(8,128)(2,1)S(1)}, bf16[2,128,128]{2,1,0:T(8,128)(2,1)}, u32[]{:S(2)}) copy-start(bf16[2,128,128]{2,1,0:T(8,128)(2,1)} %param.18) | copy-start | bytes 196612
  133.4 72.3 %all-reduce.3.cloned.1.call-start = ((), (), s32[]{:S(2)}) async-start(), calls=%async_computation.4 | async-start | bytes 524288 | tf_op jit(solution)/shard_map/psum | solution.py:114
  141.1 29.8 %copy-start.3 = (bf16[1536,128]{1,0:T(8,128)(2,1)S(1)}, bf16[1536,128]{1,0:T(8,128)(2,1)}, u32[]{:S(2)}) copy-start(bf16[1536,128]{1,0:T(8,128)(2,1)} %param.21) | copy-start | bytes 1179652
  143.9 28.0 %copy-start.12 = (bf16[2,128,128]{2,1,0:T(8,128)(2,1)S(1)}, bf16[2,128,128]{2,1,0:T(8,128)(2,1)}, u32[]{:S(2)}) copy-start(bf16[2,128,128]{2,1,0:T(8,128)(2,1)} %param.19) | copy-start | bytes 196612
  144.0 28.0 %copy-start.16 = (f32[128]{0:T(128)S(1)}, f32[128]{0:T(128)}, u32[]{:S(2)}) copy-start(f32[128]{0:T(128)} %get-tuple-element.655) | copy-start | bytes 1540
Sparse Core Ops, SparseCore 0:
  27.0 22.4 reduce-scatter.2
  133.6 23.6 reduce-scatter.4
  172.1 33.5 all-reduce.2
where the time goes:
time: 219 us; the launch traced here: 215 us
  waiting for transfers between devices  55.7 us (25%)
  matrix products  48 us (22%)
  blocking collectives  44 us (20%)
  local copies, waits for them, and re-layouts  25.7 us (12%)
  starting transfers between devices  20.9 us (10%)
  between operations  14 us (6%)
  other arithmetic  6.95 us (3%)
    psum x1, waiting for transfers between devices, shards(): lax.psum((jnp.stack([self_zero, self_one]), jnp.stack([neigh_zero, neigh_...  32.7 us
    all_gather x2, blocking collectives, over_rep(): lax.all_gather(my_part.astype(jnp.bfloat16), 'rep', axis=0, tiled=True)  24.8 us
    ppermute x9, starting transfers between devices, from_behind(): return lax.ppermute(block, axis, route)  20.8 us
    all_gather x1, blocking collectives, shards(): lax.all_gather(dh_share, 'rep', axis=1, tiled=True).reshape(feats.shape)  12.8 us
    dot_general x4, matrix products, target_term(): jnp.einsum('rkc,rkjf->cjf', chosen.astype(jnp.float32), product, precisio...  12.7 us
    reduce_scatter x2, waiting for transfers between devices, over_rep(): lax.psum_scatter(partial_value, 'rep', scatter_dimension=0, tiled=True)  12 us
    ppermute x9, waiting for transfers between devices, from_behind(): return lax.ppermute(block, axis, route)  10.9 us
    dot_general x8, matrix products, source_term(): jnp.einsum('rkji,rkjf->rif', tile_group, picked, preferred_element_type=j...  10.3 us
  transfers between devices with their start and end apart: 12, of which 5 were waited for; matrix products, arithmetic and copies ran while one was open for 26% of the time, Pallas kernels for 0%

commit v1 on v0

v1 whole, which is shorter than its diff:
```python
import functools

import jax
import jax.numpy as jnp
from jax import lax
from jax.experimental import pallas as pl
from jax.experimental.pallas import tpu as pltpu
from jax.sharding import PartitionSpec as P

MESH = pl.DeviceIdType.MESH
F32 = jnp.float32
BF16 = jnp.bfloat16


def contract(a, b, a_dim, b_dim):
    return lax.dot_general(a, b, (((a_dim,), (b_dim,)), ((), ())), preferred_element_type=F32)


def kernel(
    n_blk,
    n_rep,
    feats,
    tiles,
    col_local,
    tile_count,
    w_self,
    w_neigh,
    bias,
    cot,
    logits,
    grad_self,
    grad_neigh,
    grad_bias,
    dense,
    dense_t,
    z0_keep,
    agg_keep,
    x_in,
    spread_out,
    spread_in,
    agg_out,
    agg_in,
    logits_in,
    part_a,
    part_b,
    blk_in_a,
    blk_in_b,
    half_a,
    half_b,
    rep_in_a,
    rep_in_b,
    full_a,
    full_b,
    x_send,
    x_recv,
    spread_send,
    spread_recv,
    agg_send,
    agg_recv,
    logits_send,
    logits_recv,
    grad_send,
    grad_recv,
):
    row_blocks, slots, share, edge = tiles.shape
    slot_count = slots // n_blk
    width = feats.shape[-1]
    rows = row_blocks * share
    nodes = row_blocks * edge
    piece = width // n_blk
    blk = lax.axis_index("blk")
    rep = lax.axis_index("rep")
    whole_tiles = share % 16 == 0

    def flat(value):
        if whole_tiles:
            return value.reshape(-1, value.shape[-1]).astype(BF16)
        return value.astype(F32).reshape(-1, value.shape[-1]).astype(BF16)

    def blocks_of(value):
        if whole_tiles:
            return value.reshape(row_blocks, share, width)
        return value.astype(F32).reshape(row_blocks, share, width).astype(BF16)

    sends = []

    def send(source, target, send_sem, recv_sem, axis, partner):
        copy = pltpu.make_async_remote_copy(
            src_ref=source,
            dst_ref=target,
            send_sem=send_sem,
            recv_sem=recv_sem,
            device_id={axis: partner},
            device_id_type=MESH,
        )
        copy.start()
        sends.append(copy)
        return copy

    blk_to = [lax.rem(blk + d, n_blk) for d in range(n_blk)]
    rep_to = [lax.rem(rep + d, n_rep) for d in range(n_rep)]

    barrier = pltpu.get_barrier_semaphore()
    for d in range(1, n_blk):
        pl.semaphore_signal(barrier, inc=1, device_id={"blk": blk_to[d]}, device_id_type=MESH)
    for d in range(1, n_rep):
        pl.semaphore_signal(barrier, inc=1, device_id={"rep": rep_to[d]}, device_id_type=MESH)

    feats_share = flat(feats[:, rep])
    cot_share = flat(cot[:, rep])
    x_in[0, blk] = feats_share
    pl.semaphore_wait(barrier, n_blk - 1 + n_rep - 1)

    def share_out(layer):
        mine = x_in.at[layer, blk]
        return [
            send(mine, mine, x_send.at[layer, d], x_recv.at[layer, d], "blk", blk_to[d])
            for d in range(1, n_blk)
        ]

    arriving = share_out(0)

    unit_row = lax.broadcasted_iota(jnp.int32, (edge, edge), 0)
    unit_col = lax.broadcasted_iota(jnp.int32, (edge, edge), 1)
    unit = jnp.where(unit_row == unit_col, 1.0, 0.0).astype(BF16)

    @pl.loop(0, row_blocks)
    def _(r):
        lanes = pl.ds(pl.multiple_of(r * edge, edge), edge)
        for s in range(n_blk):
            count = tile_count[r, s]
            named = [
                jnp.where(k < count, col_local[r, s * slot_count + k], -1)
                for k in range(slot_count)
            ]
            for c in range(row_blocks):
                slot = jnp.int32(-1)
                for k in range(slot_count):
                    slot = jnp.where(named[k] == c, s * slot_count + k, slot)
                tile = tiles[r, jnp.maximum(slot, 0)].astype(dense.dtype)
                dense[s * row_blocks + c, :, lanes] = jnp.where(slot >= 0, tile, jnp.zeros_like(tile))
        turned = contract(unit, flat(dense[:, :, lanes]), 1, 1).astype(dense_t.dtype)
        for q in range(n_rep):
            dense_t[q, r] = turned[q * share : (q + 1) * share]

    def aggregate(layer, arriving):
        for copy in arriving:
            copy.wait_recv()
        x = x_in[layer].reshape(n_blk * rows, width)

        copies = []
        for d in range(1, n_rep):
            part = jnp.dot(flat(dense_t[rep_to[d]]), x, preferred_element_type=F32)
            agg_out[layer, d - 1] = part.astype(BF16)
            copies.append(
                send(
                    agg_out.at[layer, d - 1],
                    agg_in.at[layer, d - 1],
                    agg_send.at[layer, d],
                    agg_recv.at[layer, d],
                    "rep",
                    rep_to[d],
                )
            )
        agg_keep[...] = jnp.dot(flat(dense_t[rep]), x, preferred_element_type=F32)
        return copies

    def finish_aggregate(layer, copies):
        total = agg_keep[...]
        for d, copy in enumerate(copies):
            copy.wait_recv()
            total = total + agg_in[layer, d].astype(F32)
        return total.astype(BF16)

    summing = aggregate(0, arriving)

    back = contract(flat(cot[...].reshape(row_blocks * n_rep, share, width)), w_neigh[1], 1, 1).astype(BF16)
    spreading = []
    for d in range(1, n_blk):
        to = dense[pl.ds(blk_to[d] * row_blocks, row_blocks)]
        spread_out[d - 1] = jnp.dot(flat(to), back, preferred_element_type=F32).astype(BF16)
        spreading.append(
            send(
                spread_out.at[d - 1],
                spread_in.at[d - 1],
                spread_send.at[d],
                spread_recv.at[d],
                "blk",
                blk_to[d],
            )
        )
    own = dense[pl.ds(blk * row_blocks, row_blocks)]
    hidden_grad = jnp.dot(flat(own), back, preferred_element_type=F32) + contract(
        cot_share, w_self[1], 1, 1
    )

    z0_part = jnp.dot(feats_share, w_self[0], preferred_element_type=F32) + bias[0:1]
    agg0 = finish_aggregate(0, summing)
    z0 = z0_part + jnp.dot(agg0, w_neigh[0], preferred_element_type=F32)
    sigma = 1.0 / (1.0 + jnp.exp(-z0))
    h1 = (z0 * sigma).astype(BF16)
    x_in[1, blk] = h1
    arriving = share_out(1)

    for d, copy in enumerate(spreading):
        copy.wait_recv()
        hidden_grad = hidden_grad + spread_in[d].astype(F32)
    dh1 = hidden_grad.astype(BF16).astype(F32)
    dz0 = (dh1 * sigma * (1.0 + z0 * (1.0 - sigma))).astype(BF16)

    def place(part, at, value):
        for q in range(n_blk):
            part[q, at * piece : (at + 1) * piece] = value[q * piece : (q + 1) * piece]

    place(part_a, 0, contract(feats_share, dz0, 0, 0))
    place(part_a, 1, contract(agg0, dz0, 0, 0))
    place(part_a, 2, contract(h1, cot_share, 0, 0))
    bias_rows = jnp.concatenate(
        [
            jnp.sum(dz0.astype(F32), axis=0, keepdims=True),
            jnp.sum(cot_share.astype(F32), axis=0, keepdims=True),
            jnp.zeros((6, width), F32),
        ],
        axis=0,
    )
    for q in range(n_blk):
        part_a[q, 3 * piece :] = bias_rows

    def scatter_blk(which, part, blk_in):
        return [
            send(
                part.at[blk_to[d]],
                blk_in.at[d - 1],
                grad_send.at[which, 0, d],
                grad_recv.at[which, 0, d],
                "blk",
                blk_to[d],
            )
            for d in range(1, n_blk)
        ]

    def swap_rep(which, part, blk_in, half, rep_in, copies):
        total = part[blk]
        for d, copy in enumerate(copies):
            copy.wait_recv()
            total = total + blk_in[d]
        half[...] = total
        return [
            send(
                half,
                rep_in.at[d - 1],
                grad_send.at[which, 1, d],
                grad_recv.at[which, 1, d],
                "rep",
                rep_to[d],
            )
            for d in range(1, n_rep)
        ]

    def gather_blk(which, half, rep_in, full, copies):
        for copy in copies:
            copy.wait_recv()
        rep_in[n_rep - 1] = half[...]

        def of(q):
            return rep_in[lax.rem(rep + 2 * n_rep - 1 - q, n_rep)]

        total = of(0)
        for q in range(1, n_rep):
            total = total + of(q)
        full[blk] = total
        return [
            send(
                full.at[blk],
                full.at[blk],
                grad_send.at[which, 2, d],
                grad_recv.at[which, 2, d],
                "blk",
                blk_to[d],
            )
            for d in range(1, n_blk)
        ]

    grads_a = scatter_blk(0, part_a, blk_in_a)

    summing = aggregate(1, arriving)
    grads_a = swap_rep(0, part_a, blk_in_a, half_a, rep_in_a, grads_a)
    z1_part = jnp.dot(h1, w_self[1], preferred_element_type=F32) + bias[1:2]

    agg1 = finish_aggregate(1, summing)
    z1 = z1_part + jnp.dot(agg1, w_neigh[1], preferred_element_type=F32)
    logits_in[rep] = z1.astype(BF16)
    gathering = [
        send(
            logits_in.at[rep],
            logits_in.at[rep],
            logits_send.at[d],
            logits_recv.at[d],
            "rep",
            rep_to[d],
        )
        for d in range(1, n_rep)
    ]
    place(part_b, 0, contract(agg1, cot_share, 0, 0))
    grads_b = scatter_blk(1, part_b, blk_in_b)
    grads_a = gather_blk(0, half_a, rep_in_a, full_a, grads_a)
    grads_b = swap_rep(1, part_b, blk_in_b, half_b, rep_in_b, grads_b)
    grads_b = gather_blk(1, half_b, rep_in_b, full_b, grads_b)

    for copy in grads_a:
        copy.wait_recv()
    for q in range(n_blk):
        at = slice(q * piece, (q + 1) * piece)
        grad_self[0, at] = full_a[q, 0:piece]
        grad_neigh[0, at] = full_a[q, piece : 2 * piece]
        grad_self[1, at] = full_a[q, 2 * piece : 3 * piece]
    grad_bias[...] = full_a[0, 3 * piece : 3 * piece + 2]

    for copy in grads_b:
        copy.wait_recv()
    for q in range(n_blk):
        grad_neigh[1, q * piece : (q + 1) * piece] = full_b[q]
    for copy in gathering:
        copy.wait_recv()
    for q in range(n_rep):
        logits[:, q] = blocks_of(logits_in[q])
    for copy in sends:
        copy.wait_send()


def solution(mesh):
    n_blk, n_rep = mesh.shape["blk"], mesh.shape["rep"]

    def shards(feats, tiles, col_local, tile_count, w_self, w_neigh, bias, cotangent):
        row_blocks, slots, share, edge = tiles.shape
        width = feats.shape[1]
        rows = row_blocks * share
        piece = width // n_blk
        held = BF16 if share % 16 == 0 else F32
        vmem = pl.BlockSpec(memory_space=pltpu.VMEM)
        smem = pl.BlockSpec(memory_space=pltpu.SMEM)
        split = (row_blocks, n_rep, share, width)
        dma = pltpu.SemaphoreType.DMA
        a_rows, b_rows = 3 * piece + 8, piece
        logits, grad_self, grad_neigh, grad_bias = pl.pallas_call(
            functools.partial(kernel, n_blk, n_rep),
            out_shape=(
                jax.ShapeDtypeStruct(split, BF16),
                jax.ShapeDtypeStruct((2, width, width), F32),
                jax.ShapeDtypeStruct((2, width, width), F32),
                jax.ShapeDtypeStruct((2, width), F32),
            ),
            in_specs=[vmem, vmem, smem, smem, vmem, vmem, vmem, vmem],
            out_specs=(vmem, vmem, vmem, vmem),
            scratch_shapes=[
                pltpu.VMEM((n_blk * row_blocks, share, row_blocks * edge), held),
                pltpu.VMEM((n_rep, row_blocks, share, n_blk * rows), held),
                pltpu.VMEM((rows, width), F32),
                pltpu.VMEM((rows, width), F32),
                pltpu.VMEM((2, n_blk, rows, width), BF16),
                pltpu.VMEM((n_blk - 1, rows, width), BF16),
                pltpu.VMEM((n_blk - 1, rows, width), BF16),
                pltpu.VMEM((2, n_rep - 1, rows, width), BF16),
                pltpu.VMEM((2, n_rep - 1, rows, width), BF16),
                pltpu.VMEM((n_rep, rows, width), BF16),
                pltpu.VMEM((n_blk, a_rows, width), F32),
                pltpu.VMEM((n_blk, b_rows, width), F32),
                pltpu.VMEM((n_blk - 1, a_rows, width), F32),
                pltpu.VMEM((n_blk - 1, b_rows, width), F32),
                pltpu.VMEM((a_rows, width), F32),
                pltpu.VMEM((b_rows, width), F32),
                pltpu.VMEM((n_rep, a_rows, width), F32),
                pltpu.VMEM((n_rep, b_rows, width), F32),
                pltpu.VMEM((n_blk, a_rows, width), F32),
                pltpu.VMEM((n_blk, b_rows, width), F32),
                dma((2, n_blk)),
                dma((2, n_blk)),
                dma((n_blk,)),
                dma((n_blk,)),
                dma((2, n_rep)),
                dma((2, n_rep)),
                dma((n_rep,)),
                dma((n_rep,)),
                dma((2, 3, max(n_blk, n_rep))),
                dma((2, 3, max(n_blk, n_rep))),
            ],
            compiler_params=pltpu.CompilerParams(
                collective_id=0, has_side_effects=True, vmem_limit_bytes=52 * 2**20
            ),
        )(
            feats.reshape(split),
            tiles,
            col_local,
            tile_count,
            w_self,
            w_neigh,
            bias,
            cotangent.reshape(split),
        )
        return logits.reshape(feats.shape), grad_self, grad_neigh, grad_bias

    return jax.shard_map(
        shards,
        mesh=mesh,
        in_specs=(
            P(("group", "blk"), None),
            P(("group", "blk"), None, "rep", None),
            P(("group", "blk"), None),
            P(("group", "blk"), None),
            P(),
            P(),
            P(),
            P(("group", "blk"), None),
        ),
        out_specs=(
            P(("group", "blk"), None),
            P("group", None, None),
            P("group", None, None),
            P("group", None),
        ),
        check_vma=False,
    )
```

time: 219 us -> 69.4 us (0.32); the launches traced: 215 us -> 68.6 us
  Pallas kernels: 0 us -> 59.5 us
  waiting for transfers between devices: 55.7 us -> 0 us
  matrix products: 48 us -> 0 us
  blocking collectives: 44 us -> 0 us
  starting transfers between devices: 20.9 us -> 0 us
  local copies, waits for them, and re-layouts: 25.7 us -> 8.43 us
  between operations: 14 us -> 0.65 us
  other arithmetic: 6.95 us -> 0 us
    pallas_call x0 -> x1, Pallas kernels: none -> 59.5 us  [shards(): pl.pallas_call(functools.partial(kernel, n_blk, n_rep), out_shape=(jax.Sh...]
    dot_general x34 -> x0, matrix products: 48 us -> none  [the longest x4 12.7 us: target_term(): jnp.einsum('rkc,rkjf->cjf', chosen.astype(jnp.float32), product, precisio...]
    all_gather x3 -> x0, blocking collectives: 37.6 us -> none  [the longest x2 24.8 us: over_rep(): lax.all_gather(my_part.astype(jnp.bfloat16), 'rep', axis=0, tiled=True)]
    psum x1 -> x0, waiting for transfers between devices: 32.7 us -> none  [shards(): lax.psum((jnp.stack([self_zero, self_one]), jnp.stack([neigh_zero, neigh_...]
    ppermute x9 -> x0, starting transfers between devices: 20.8 us -> none  [from_behind(): return lax.ppermute(block, axis, route)]
    dynamic_slice x23 -> x0, local copies, waits for them, and re-layouts: 14.3 us -> none  [the longest x10 7.47 us: selector_for(): counts = lax.dynamic_slice_in_dim(tile_count, source, 1, 1)]
    reduce_scatter x2 -> x0, waiting for transfers between devices: 12 us -> none  [over_rep(): lax.psum_scatter(partial_value, 'rep', scatter_dimension=0, tiled=True)]
    ppermute x9 -> x0, waiting for transfers between devices: 10.9 us -> none  [from_behind(): return lax.ppermute(block, axis, route)]
  transfers between devices with their start and end apart: 12 -> 0, of which waited for: 5 -> 0; matrix products, arithmetic and copies ran while one was open for 26% -> 0% of each run, Pallas kernels for 0% -> 0%
where the time goes in v1:
time: 69.4 us; the launch traced here: 68.6 us
  Pallas kernels  59.5 us (86%)
  local copies, waits for them, and re-layouts  8.43 us (12%)
    pallas_call x1, Pallas kernels, shards(): pl.pallas_call(functools.partial(kernel, n_blk, n_rep), out_shape=(jax.Sh...  59.5 us
    unnamed x17, local copies, waits for them, and re-layouts  8.43 us

profile of v1, /device:TPU:1, one launch (start us, length us, event | category | flops | bytes accessed | tf_op | source)
XLA Modules:
  0.0 68.6 jit_solution(12294502312906801187)
XLA Ops:
  0.6 0.8 %copy.12.tile_count = s32[12,4]{1,0:T(8,128)S(1)} copy(s32[12,4]{0,1:T(4,128)} %param.11) | data formatting | bytes 384 | tf_op args[3]
  1.4 0.0 copy-start
  1.4 1.0 %copy-done = bf16[1536,128]{1,0:T(8,128)(2,1)S(1)} copy-done((bf16[1536,128]{1,0:T(8,128)(2,1)S(1)}, bf16[1536,128]{1,0:T(8,128)(2,1)}, u32[]{:S(2)}) %copy-start) | copy-done | bytes 393240
  2.4 0.0 copy-start.1
  2.4 1.0 %copy-done.1 = bf16[1536,128]{1,0:T(8,128)(2,1)S(1)} copy-done((bf16[1536,128]{1,0:T(8,128)(2,1)S(1)}, bf16[1536,128]{1,0:T(8,128)(2,1)}, u32[]{:S(2)}) %copy-start.1) | copy-done | bytes 393240
  3.4 0.0 copy-start.2
  3.4 0.8 %copy-done.2 = bf16[2,128,128]{2,1,0:T(8,128)(2,1)S(1)} copy-done((bf16[2,128,128]{2,1,0:T(8,128)(2,1)S(1)}, bf16[2,128,128]{2,1,0:T(8,128)(2,1)}, u32[]{:S(2)}) %copy-start.2) | copy-done | bytes 65560
  4.2 0.0 copy-start.3
  4.2 0.8 %copy-done.3 = bf16[2,128,128]{2,1,0:T(8,128)(2,1)S(1)} copy-done((bf16[2,128,128]{2,1,0:T(8,128)(2,1)S(1)}, bf16[2,128,128]{2,1,0:T(8,128)(2,1)}, u32[]{:S(2)}) %copy-start.3) | copy-done | bytes 65560
  5.1 0.0 copy-start.4
  5.1 0.7 %copy-done.4 = s32[12,24]{1,0:T(8,128)S(1)} copy-done((s32[12,24]{1,0:T(8,128)S(1)}, s32[12,24]{1,0:T(8,128)}, u32[]{:S(2)}) %copy-start.4) | copy-done | bytes 1176
  5.8 0.0 copy-start.5
  5.8 0.7 copy-done.5
  6.5 59.5 %shard_map.111 = (bf16[12,4,32,128]{3,2,1,0:T(8,128)(2,1)S(1)}, f32[2,128,128]{2,1,0:T(8,128)S(1)}, f32[2,128,128]{2,1,0:T(8,128)S(1)}, f32[2,128]{1,0:T(2,128)S(1)}) custom-call(bf16[12,4,32,128]{3,2,1,0:T(8,128)(2,1)S(1)} %bitcast.3, bf16[12,24,32,128]{3,2,1,0:T(8,128)(2,1)} %tiles.1, s32[12,24]{1,0:T(8,128)S(1)} %copy-done.4, ...), custom_call_target="tpu_custom_call" | custom-call | tf_op jit(solution)/shard_map/pallas_call | solution.py:345
  66.0 0.7 %copy.17 = bf16[1536,128]{1,0:T(8,128)(2,1)} copy(bf16[1536,128]{1,0:T(8,128)(2,1)S(1)} %bitcast.5) | data formatting | bytes 786432
  66.8 0.7 copy.18
  67.4 0.7 copy.19
  68.1 0.6 copy.20
Async XLA Ops:
  1.4 1.0 %copy-start = (bf16[1536,128]{1,0:T(8,128)(2,1)S(1)}, bf16[1536,128]{1,0:T(8,128)(2,1)}, u32[]{:S(2)}) copy-start(bf16[1536,128]{1,0:T(8,128)(2,1)} %param.8) | copy-start | bytes 1179652
  2.4 1.0 %copy-start.1 = (bf16[1536,128]{1,0:T(8,128)(2,1)S(1)}, bf16[1536,128]{1,0:T(8,128)(2,1)}, u32[]{:S(2)}) copy-start(bf16[1536,128]{1,0:T(8,128)(2,1)} %param.15) | copy-start | bytes 1179652
  3.4 0.8 %copy-start.2 = (bf16[2,128,128]{2,1,0:T(8,128)(2,1)S(1)}, bf16[2,128,128]{2,1,0:T(8,128)(2,1)}, u32[]{:S(2)}) copy-start(bf16[2,128,128]{2,1,0:T(8,128)(2,1)} %w_self.1) | copy-start | bytes 196612
  4.2 0.8 %copy-start.3 = (bf16[2,128,128]{2,1,0:T(8,128)(2,1)S(1)}, bf16[2,128,128]{2,1,0:T(8,128)(2,1)}, u32[]{:S(2)}) copy-start(bf16[2,128,128]{2,1,0:T(8,128)(2,1)} %w_neigh.1) | copy-start | bytes 196612
  5.1 0.7 %copy-start.4 = (s32[12,24]{1,0:T(8,128)S(1)}, s32[12,24]{1,0:T(8,128)}, u32[]{:S(2)}) copy-start(s32[12,24]{1,0:T(8,128)} %col_local.1) | copy-start | bytes 3460
  5.8 0.7 copy-start.5

commit v2 on v1

v2 whole, which is shorter than its diff:
```python
import functools

import jax
import jax.numpy as jnp
from jax import lax
from jax.experimental import pallas as pl
from jax.experimental.pallas import tpu as pltpu
from jax.sharding import PartitionSpec as P

MESH = pl.DeviceIdType.MESH
F32 = jnp.float32
BF16 = jnp.bfloat16
HALVES = 2


def contract(a, b, a_dim, b_dim):
    return lax.dot_general(a, b, (((a_dim,), (b_dim,)), ((), ())), preferred_element_type=F32)


def kernel(
    n_blk,
    n_rep,
    feats_hbm,
    tiles_hbm,
    col_hbm,
    count_hbm,
    w_self_hbm,
    w_neigh_hbm,
    bias_hbm,
    cot_hbm,
    logits,
    grad_self,
    grad_neigh,
    grad_bias,
    feats,
    tiles,
    col_local,
    tile_count,
    w_self,
    w_neigh,
    bias,
    cot,
    dense,
    dense_t,
    agg_keep,
    x_in,
    spread_out,
    spread_in,
    agg_out,
    agg_in,
    logits_in,
    part,
    blk_in,
    half,
    rep_in,
    full,
    load_sem,
    x_send,
    x_recv,
    spread_send,
    spread_recv,
    agg_send,
    agg_recv,
    logits_send,
    logits_recv,
    grad_send,
    grad_recv,
):
    row_blocks, slots, share, edge = tiles.shape
    slot_count = slots // n_blk
    width = feats.shape[-1]
    rows = row_blocks * share
    piece = width // n_blk
    n_chip = n_blk // 2
    half_blocks = row_blocks // HALVES
    half_rows = rows // HALVES
    blk = lax.axis_index("blk")
    rep = lax.axis_index("rep")
    whole_tiles = share % 16 == 0

    def flat(value):
        if whole_tiles:
            return value.reshape(-1, value.shape[-1]).astype(BF16)
        return value.astype(F32).reshape(-1, value.shape[-1]).astype(BF16)

    def blocks_of(value):
        if whole_tiles:
            return value.reshape(row_blocks, share, width)
        return value.astype(F32).reshape(row_blocks, share, width).astype(BF16)

    sends = []

    def send(source, target, send_sem, recv_sem, axis, partner):
        copy = pltpu.make_async_remote_copy(
            src_ref=source,
            dst_ref=target,
            send_sem=send_sem,
            recv_sem=recv_sem,
            device_id={axis: partner},
            device_id_type=MESH,
        )
        copy.start()
        sends.append(copy)
        return copy

    blk_to = [lax.rem(blk + d, n_blk) for d in range(n_blk)]
    rep_to = [lax.rem(rep + d, n_rep) for d in range(n_rep)]
    core = lax.rem(blk, 2)
    mate = blk + 1 - 2 * core

    barrier = pltpu.get_barrier_semaphore()
    for d in range(1, n_blk):
        pl.semaphore_signal(barrier, inc=1, device_id={"blk": blk_to[d]}, device_id_type=MESH)
    for d in range(1, n_rep):
        pl.semaphore_signal(barrier, inc=1, device_id={"rep": rep_to[d]}, device_id_type=MESH)

    pairs = [
        (feats_hbm, feats),
        (col_hbm, col_local),
        (count_hbm, tile_count),
        (tiles_hbm, tiles),
        (cot_hbm, cot),
        (w_self_hbm, w_self),
        (w_neigh_hbm, w_neigh),
        (bias_hbm, bias),
    ]
    loads = [pltpu.make_async_copy(a, b, load_sem.at[i]) for i, (a, b) in enumerate(pairs)]
    for load in loads:
        load.start()
    loads[0].wait()
    feats_share = flat(feats[:, rep])
    x_in[0, blk] = feats_share
    pl.semaphore_wait(barrier, n_blk - 1 + n_rep - 1)

    def span(h):
        return pl.ds(h * half_rows, half_rows)

    def share_out(layer, h):
        mine = x_in.at[layer, blk, span(h)]
        out = []
        for d in range(1, n_chip):
            to = lax.rem(blk + 2 * d, n_blk)
            out.append(send(mine, mine, x_send.at[layer, h, d], x_recv.at[layer, h, d], "blk", to))
        near = send(mine, mine, x_send.at[layer, h, 0], x_recv.at[layer, h, 0], "blk", mate)
        return out, near

    def pass_on(layer, h, arriving):
        out, near = arriving
        passed = [near]
        for d in range(1, n_chip):
            out[d - 1].wait_recv()
            source = lax.rem(blk + n_blk - 2 * d, n_blk)
            theirs = x_in.at[layer, source, span(h)]
            at = n_chip + d - 1
            passed.append(
                send(theirs, theirs, x_send.at[layer, h, at], x_recv.at[layer, h, at], "blk", mate)
            )
        return passed

    arriving = [share_out(0, h) for h in range(HALVES)]

    unit_row = lax.broadcasted_iota(jnp.int32, (edge, edge), 0)
    unit_col = lax.broadcasted_iota(jnp.int32, (edge, edge), 1)
    unit = jnp.where(unit_row == unit_col, 1.0, 0.0).astype(BF16)
    for load in loads[1:4]:
        load.wait()

    def densify(first, last):
        @pl.loop(first, last)
        def _(r):
            lanes = pl.ds(pl.multiple_of(r * edge, edge), edge)
            for s in range(n_blk):
                count = tile_count[r, s]
                named = [
                    jnp.where(k < count, col_local[r, s * slot_count + k], -1)
                    for k in range(slot_count)
                ]
                for c in range(row_blocks):
                    slot = jnp.int32(-1)
                    for k in range(slot_count):
                        slot = jnp.where(named[k] == c, s * slot_count + k, slot)
                    tile = tiles[r, jnp.maximum(slot, 0)].astype(dense.dtype)
                    dense[s * row_blocks + c, :, lanes] = jnp.where(
                        slot >= 0, tile, jnp.zeros_like(tile)
                    )
            turned = contract(unit, flat(dense[:, :, lanes]), 1, 1).astype(dense_t.dtype)
            for q in range(n_rep):
                dense_t[q, r] = turned[q * share : (q + 1) * share]

    densify(0, half_blocks)
    arriving = [pass_on(0, h, arriving[h]) for h in range(HALVES)]
    densify(half_blocks, row_blocks)
    for load in loads[4:]:
        load.wait()

    def aggregate(layer, arriving):
        for passed in arriving:
            for copy in passed:
                copy.wait_recv()
        x = x_in[layer].reshape(n_blk * rows, width)
        copies = []
        for h in range(HALVES):
            at = pl.ds(h * half_blocks, half_blocks)
            of_half = []
            for d in range(1, n_rep):
                part = jnp.dot(flat(dense_t[rep_to[d], at]), x, preferred_element_type=F32)
                agg_out[layer, d - 1, span(h)] = part.astype(BF16)
                of_half.append(
                    send(
                        agg_out.at[layer, d - 1, span(h)],
                        agg_in.at[layer, d - 1, span(h)],
                        agg_send.at[layer, h, d],
                        agg_recv.at[layer, h, d],
                        "rep",
                        rep_to[d],
                    )
                )
            copies.append(of_half)
        agg_keep[...] = jnp.dot(flat(dense_t[rep]), x, preferred_element_type=F32)
        return copies

    def finish_aggregate(layer, h, copies):
        total = agg_keep[span(h)]
        for d, copy in enumerate(copies[h]):
            copy.wait_recv()
            total = total + agg_in[layer, d, span(h)].astype(F32)
        return total.astype(BF16)

    summing = aggregate(0, arriving)

    cot_share = flat(cot[:, rep])
    back = contract(flat(cot[...].reshape(row_blocks * n_rep, share, width)), w_neigh[1], 1, 1).astype(BF16)
    spreading = []
    for d in range(1, n_blk):
        to = dense[pl.ds(blk_to[d] * row_blocks, row_blocks)]
        spread_out[d - 1] = jnp.dot(flat(to), back, preferred_element_type=F32).astype(BF16)
        spreading.append(
            send(
                spread_out.at[d - 1],
                spread_in.at[d - 1],
                spread_send.at[d],
                spread_recv.at[d],
                "blk",
                blk_to[d],
            )
        )
    own = dense[pl.ds(blk * row_blocks, row_blocks)]
    hidden_grad = jnp.dot(flat(own), back, preferred_element_type=F32) + contract(
        cot_share, w_self[1], 1, 1
    )

    z0_part = jnp.dot(feats_share, w_self[0], preferred_element_type=F32) + bias[0:1]
    agg0, z0, sigma, arriving = [], [], [], []
    for h in range(HALVES):
        at = slice(h * half_rows, (h + 1) * half_rows)
        agg0.append(finish_aggregate(0, h, summing))
        z0.append(z0_part[at] + jnp.dot(agg0[h], w_neigh[0], preferred_element_type=F32))
        sigma.append(1.0 / (1.0 + jnp.exp(-z0[h])))
        x_in[1, blk, span(h)] = (z0[h] * sigma[h]).astype(BF16)
        arriving.append(share_out(1, h))
    agg0 = jnp.concatenate(agg0, axis=0)
    z0 = jnp.concatenate(z0, axis=0)
    sigma = jnp.concatenate(sigma, axis=0)
    h1 = x_in[1, blk]
    arriving[0] = pass_on(1, 0, arriving[0])

    for d, copy in enumerate(spreading):
        copy.wait_recv()
        hidden_grad = hidden_grad + spread_in[d].astype(F32)
    dh1 = hidden_grad.astype(BF16).astype(F32)
    dz0 = (dh1 * sigma * (1.0 + z0 * (1.0 - sigma))).astype(BF16)
    for h in range(1, HALVES):
        arriving[h] = pass_on(1, h, arriving[h])

    summing = aggregate(1, arriving)

    def place(at, value):
        for q in range(n_blk):
            part[q, at * piece : (at + 1) * piece] = value[q * piece : (q + 1) * piece]

    place(0, contract(feats_share, dz0, 0, 0))
    place(1, contract(agg0, dz0, 0, 0))
    place(2, contract(h1, cot_share, 0, 0))
    neigh_one = contract(agg_keep[...].astype(BF16), cot_share, 0, 0)
    for d in range(1, n_rep):
        neigh_one = neigh_one + contract(agg_out[1, d - 1], flat(cot[:, rep_to[d]]), 0, 0)
    place(3, neigh_one)
    bias_rows = jnp.concatenate(
        [
            jnp.sum(dz0.astype(F32), axis=0, keepdims=True),
            jnp.sum(cot_share.astype(F32), axis=0, keepdims=True),
            jnp.zeros((14, width), F32),
        ],
        axis=0,
    )
    for q in range(n_blk):
        part[q, 4 * piece :] = bias_rows
    scattering = [
        send(
            part.at[blk_to[d]],
            blk_in.at[d - 1],
            grad_send.at[0, d],
            grad_recv.at[0, d],
            "blk",
            blk_to[d],
        )
        for d in range(1, n_blk)
    ]
    z1_part = jnp.dot(h1, w_self[1], preferred_element_type=F32) + bias[1:2]

    total = part[blk]
    for d, copy in enumerate(scattering):
        copy.wait_recv()
        total = total + blk_in[d]
    half[...] = total.astype(BF16)
    swapping = [
        send(
            half,
            rep_in.at[d - 1],
            grad_send.at[1, d],
            grad_recv.at[1, d],
            "rep",
            rep_to[d],
        )
        for d in range(1, n_rep)
    ]

    gathering = []
    for h in range(HALVES):
        at = slice(h * half_rows, (h + 1) * half_rows)
        agg1 = finish_aggregate(1, h, summing)
        z1 = z1_part[at] + jnp.dot(agg1, w_neigh[1], preferred_element_type=F32)
        logits_in[rep, span(h)] = z1.astype(BF16)
        gathering += [
            send(
                logits_in.at[rep, span(h)],
                logits_in.at[rep, span(h)],
                logits_send.at[h, d],
                logits_recv.at[h, d],
                "rep",
                rep_to[d],
            )
            for d in range(1, n_rep)
        ]

    for copy in swapping:
        copy.wait_recv()
    rep_in[n_rep - 1] = half[...]

    def of(q):
        return rep_in[lax.rem(rep + 2 * n_rep - 1 - q, n_rep)].astype(F32)

    total = of(0)
    for q in range(1, n_rep):
        total = total + of(q)
    full[blk] = total
    spreading_out = [
        send(
            full.at[blk],
            full.at[blk],
            grad_send.at[2, d],
            grad_recv.at[2, d],
            "blk",
            blk_to[d],
        )
        for d in range(1, n_blk)
    ]
    for copy in spreading_out:
        copy.wait_recv()
    for q in range(n_blk):
        at = slice(q * piece, (q + 1) * piece)
        grad_self[0, at] = full[q, 0:piece]
        grad_neigh[0, at] = full[q, piece : 2 * piece]
        grad_self[1, at] = full[q, 2 * piece : 3 * piece]
        grad_neigh[1, at] = full[q, 3 * piece : 4 * piece]
    grad_bias[...] = full[0, 4 * piece : 4 * piece + 2]

    for copy in gathering:
        copy.wait_recv()
    for q in range(n_rep):
        logits[:, q] = blocks_of(logits_in[q])
    for copy in sends:
        copy.wait_send()


def solution(mesh):
    n_blk, n_rep = mesh.shape["blk"], mesh.shape["rep"]

    def shards(feats, tiles, col_local, tile_count, w_self, w_neigh, bias, cotangent):
        row_blocks, slots, share, edge = tiles.shape
        width = feats.shape[1]
        rows = row_blocks * share
        piece = width // n_blk
        held = BF16 if share % 16 == 0 else F32
        vmem = pl.BlockSpec(memory_space=pltpu.VMEM)
        split = (row_blocks, n_rep, share, width)
        dma = pltpu.SemaphoreType.DMA
        grad_rows = 4 * piece + 16
        wide = max(n_blk, n_rep)
        anywhere = pl.BlockSpec(memory_space=pl.ANY)
        logits, grad_self, grad_neigh, grad_bias = pl.pallas_call(
            functools.partial(kernel, n_blk, n_rep),
            out_shape=(
                jax.ShapeDtypeStruct(split, BF16),
                jax.ShapeDtypeStruct((2, width, width), F32),
                jax.ShapeDtypeStruct((2, width, width), F32),
                jax.ShapeDtypeStruct((2, width), F32),
            ),
            in_specs=[anywhere] * 8,
            out_specs=(vmem, vmem, vmem, vmem),
            scratch_shapes=[
                pltpu.VMEM(split, BF16),
                pltpu.VMEM(tiles.shape, BF16),
                pltpu.SMEM(col_local.shape, jnp.int32),
                pltpu.SMEM(tile_count.shape, jnp.int32),
                pltpu.VMEM(w_self.shape, BF16),
                pltpu.VMEM(w_neigh.shape, BF16),
                pltpu.VMEM(bias.shape, F32),
                pltpu.VMEM(split, BF16),
                pltpu.VMEM((n_blk * row_blocks, share, row_blocks * edge), held),
                pltpu.VMEM((n_rep, row_blocks, share, n_blk * rows), held),
                pltpu.VMEM((rows, width), F32),
                pltpu.VMEM((2, n_blk, rows, width), BF16),
                pltpu.VMEM((n_blk - 1, rows, width), BF16),
                pltpu.VMEM((n_blk - 1, rows, width), BF16),
                pltpu.VMEM((2, n_rep - 1, rows, width), BF16),
                pltpu.VMEM((2, n_rep - 1, rows, width), BF16),
                pltpu.VMEM((n_rep, rows, width), BF16),
                pltpu.VMEM((n_blk, grad_rows, width), F32),
                pltpu.VMEM((n_blk - 1, grad_rows, width), F32),
                pltpu.VMEM((grad_rows, width), BF16),
                pltpu.VMEM((n_rep, grad_rows, width), BF16),
                pltpu.VMEM((n_blk, grad_rows, width), F32),
                dma((8,)),
                dma((2, HALVES, n_blk)),
                dma((2, HALVES, n_blk)),
                dma((n_blk,)),
                dma((n_blk,)),
                dma((2, HALVES, n_rep)),
                dma((2, HALVES, n_rep)),
                dma((HALVES, n_rep)),
                dma((HALVES, n_rep)),
                dma((3, wide)),
                dma((3, wide)),
            ],
            compiler_params=pltpu.CompilerParams(
                collective_id=0, has_side_effects=True, vmem_limit_bytes=52 * 2**20
            ),
        )(
            feats.reshape(split),
            tiles,
            col_local,
            tile_count,
            w_self,
            w_neigh,
            bias,
            cotangent.reshape(split),
        )
        return logits.reshape(feats.shape), grad_self, grad_neigh, grad_bias

    return jax.shard_map(
        shards,
        mesh=mesh,
        in_specs=(
            P(("group", "blk"), None),
            P(("group", "blk"), None, "rep", None),
            P(("group", "blk"), None),
            P(("group", "blk"), None),
            P(),
            P(),
            P(),
            P(("group", "blk"), None),
        ),
        out_specs=(
            P(("group", "blk"), None),
            P("group", None, None),
            P("group", None, None),
            P("group", None),
        ),
        check_vma=False,
    )
```

time: 69.4 us -> 58.3 us (0.84)
  Pallas kernels: 59.5 us -> 48.9 us
    pallas_call x1, Pallas kernels: 59.5 us -> 48.9 us  [shards(): pl.pallas_call(functools.partial(kernel, n_blk, n_rep), out_shape=(jax.Sh...]
where the time goes in v2:
time: 58.3 us; the launch traced here: 58 us
  Pallas kernels  48.9 us (84%)
  local copies, waits for them, and re-layouts  8.43 us (14%)
  between operations  0.65 us (1%)
    pallas_call x1, Pallas kernels, shards(): pl.pallas_call(functools.partial(kernel, n_blk, n_rep), out_shape=(jax.Sh...  48.9 us
    unnamed x17, local copies, waits for them, and re-layouts  8.43 us

profile of v2, /device:TPU:1, one launch (start us, length us, event | category | flops | bytes accessed | tf_op | source)
XLA Modules:
  0.0 58.0 jit_solution(15655632856346688502)
XLA Ops:
  0.6 0.8 %copy.12.count_hbm = s32[12,4]{1,0:T(8,128)S(1)} copy(s32[12,4]{0,1:T(4,128)} %param.11) | data formatting | bytes 384 | tf_op args[3]
  1.4 0.0 copy-start
  1.4 1.0 %copy-done = bf16[1536,128]{1,0:T(8,128)(2,1)S(1)} copy-done((bf16[1536,128]{1,0:T(8,128)(2,1)S(1)}, bf16[1536,128]{1,0:T(8,128)(2,1)}, u32[]{:S(2)}) %copy-start) | copy-done | bytes 393240
  2.4 0.0 copy-start.1
  2.4 1.0 %copy-done.1 = bf16[1536,128]{1,0:T(8,128)(2,1)S(1)} copy-done((bf16[1536,128]{1,0:T(8,128)(2,1)S(1)}, bf16[1536,128]{1,0:T(8,128)(2,1)}, u32[]{:S(2)}) %copy-start.1) | copy-done | bytes 393240
  3.4 0.0 copy-start.2
  3.4 0.8 %copy-done.2 = bf16[2,128,128]{2,1,0:T(8,128)(2,1)S(1)} copy-done((bf16[2,128,128]{2,1,0:T(8,128)(2,1)S(1)}, bf16[2,128,128]{2,1,0:T(8,128)(2,1)}, u32[]{:S(2)}) %copy-start.2) | copy-done | bytes 65560
  4.2 0.0 copy-start.3
  4.2 0.8 %copy-done.3 = bf16[2,128,128]{2,1,0:T(8,128)(2,1)S(1)} copy-done((bf16[2,128,128]{2,1,0:T(8,128)(2,1)S(1)}, bf16[2,128,128]{2,1,0:T(8,128)(2,1)}, u32[]{:S(2)}) %copy-start.3) | copy-done | bytes 65560
  5.1 0.0 copy-start.4
  5.1 0.7 %copy-done.4 = s32[12,24]{1,0:T(8,128)S(1)} copy-done((s32[12,24]{1,0:T(8,128)S(1)}, s32[12,24]{1,0:T(8,128)}, u32[]{:S(2)}) %copy-start.4) | copy-done | bytes 1176
  5.8 0.0 copy-start.5
  5.8 0.7 %copy-done.5 = f32[2,128]{1,0:T(2,128)S(1)} copy-done((f32[2,128]{1,0:T(2,128)S(1)}, f32[2,128]{1,0:T(2,128)}, u32[]{:S(2)}) %copy-start.5) | copy-done | bytes 1048
  6.5 48.9 %shard_map.111 = (bf16[12,4,32,128]{3,2,1,0:T(8,128)(2,1)S(1)}, f32[2,128,128]{2,1,0:T(8,128)S(1)}, f32[2,128,128]{2,1,0:T(8,128)S(1)}, f32[2,128]{1,0:T(2,128)S(1)}) custom-call(bf16[12,4,32,128]{3,2,1,0:T(8,128)(2,1)S(1)} %bitcast.3, bf16[12,24,32,128]{3,2,1,0:T(8,128)(2,1)} %tiles_hbm.1, s32[12,24]{1,0:T(8,128)S(1)} %copy-done.4, ...), custom_call_target="tpu_custom_call" | custom-call | tf_op jit(solution)/shard_map/pallas_call | solution.py:401
  55.3 0.7 %copy.17 = bf16[1536,128]{1,0:T(8,128)(2,1)} copy(bf16[1536,128]{1,0:T(8,128)(2,1)S(1)} %bitcast.5) | data formatting | bytes 786432
  56.1 0.7 %copy.18 = f32[2,128,128]{2,1,0:T(8,128)} copy(f32[2,128,128]{2,1,0:T(8,128)S(1)} %get-tuple-element.17) | data formatting | bytes 262144
  56.7 0.7 %copy.19 = f32[2,128,128]{2,1,0:T(8,128)} copy(f32[2,128,128]{2,1,0:T(8,128)S(1)} %get-tuple-element.18) | data formatting | bytes 262144
  57.4 0.6 copy.20
Async XLA Ops:
  1.4 1.0 %copy-start = (bf16[1536,128]{1,0:T(8,128)(2,1)S(1)}, bf16[1536,128]{1,0:T(8,128)(2,1)}, u32[]{:S(2)}) copy-start(bf16[1536,128]{1,0:T(8,128)(2,1)} %param.8) | copy-start | bytes 1179652
  2.4 1.0 %copy-start.1 = (bf16[1536,128]{1,0:T(8,128)(2,1)S(1)}, bf16[1536,128]{1,0:T(8,128)(2,1)}, u32[]{:S(2)}) copy-start(bf16[1536,128]{1,0:T(8,128)(2,1)} %param.15) | copy-start | bytes 1179652
  3.4 0.8 %copy-start.2 = (bf16[2,128,128]{2,1,0:T(8,128)(2,1)S(1)}, bf16[2,128,128]{2,1,0:T(8,128)(2,1)}, u32[]{:S(2)}) copy-start(bf16[2,128,128]{2,1,0:T(8,128)(2,1)} %w_self_hbm.1) | copy-start | bytes 196612
  4.2 0.8 %copy-start.3 = (bf16[2,128,128]{2,1,0:T(8,128)(2,1)S(1)}, bf16[2,128,128]{2,1,0:T(8,128)(2,1)}, u32[]{:S(2)}) copy-start(bf16[2,128,128]{2,1,0:T(8,128)(2,1)} %w_neigh_hbm.1) | copy-start | bytes 196612
  5.1 0.7 %copy-start.4 = (s32[12,24]{1,0:T(8,128)S(1)}, s32[12,24]{1,0:T(8,128)}, u32[]{:S(2)}) copy-start(s32[12,24]{1,0:T(8,128)} %col_hbm.1) | copy-start | bytes 3460
  5.8 0.7 %copy-start.5 = (f32[2,128]{1,0:T(2,128)S(1)}, f32[2,128]{1,0:T(2,128)}, u32[]{:S(2)}) copy-start(f32[2,128]{1,0:T(2,128)} %bias_hbm.1) | copy-start | bytes 3076

commit v3 on v2

--- a/solution.py
+++ b/solution.py
@@ -170,7 +170,7 @@
         def _(r):
             lanes = pl.ds(pl.multiple_of(r * edge, edge), edge)
             for s in range(n_blk):
-                count = tile_count[r, s]
+                count = tile_count[s, r]
                 named = [
                     jnp.where(k < count, col_local[r, s * slot_count + k], -1)
                     for k in range(slot_count)
@@ -398,7 +398,7 @@
         grad_rows = 4 * piece + 16
         wide = max(n_blk, n_rep)
         anywhere = pl.BlockSpec(memory_space=pl.ANY)
-        logits, grad_self, grad_neigh, grad_bias = pl.pallas_call(
+        made = pl.pallas_call(
             functools.partial(kernel, n_blk, n_rep),
             out_shape=(
                 jax.ShapeDtypeStruct(split, BF16),
@@ -412,7 +412,7 @@
                 pltpu.VMEM(split, BF16),
                 pltpu.VMEM(tiles.shape, BF16),
                 pltpu.SMEM(col_local.shape, jnp.int32),
-                pltpu.SMEM(tile_count.shape, jnp.int32),
+                pltpu.SMEM(tile_count.shape[::-1], jnp.int32),
                 pltpu.VMEM(w_self.shape, BF16),
                 pltpu.VMEM(w_neigh.shape, BF16),
                 pltpu.VMEM(bias.shape, F32),
@@ -444,18 +444,19 @@
                 dma((3, wide)),
             ],
             compiler_params=pltpu.CompilerParams(
-                collective_id=0, has_side_effects=True, vmem_limit_bytes=52 * 2**20
+                collective_id=0, has_side_effects=True, vmem_limit_bytes=64 * 2**20 - 1400 * 2**10
             ),
         )(
             feats.reshape(split),
             tiles,
             col_local,
-            tile_count,
+            tile_count.T,
             w_self,
             w_neigh,
             bias,
             cotangent.reshape(split),
         )
+        logits, grad_self, grad_neigh, grad_bias = made
         return logits.reshape(feats.shape), grad_self, grad_neigh, grad_bias
 
     return jax.shard_map(

time: 58.3 us -> 56.7 us (0.973)
  local copies, waits for them, and re-layouts: 8.43 us -> 6.12 us
  Pallas kernels: 48.9 us -> 49.8 us
    unnamed x17 -> x4, local copies, waits for them, and re-layouts: 8.43 us -> 6.12 us
    pallas_call x1, Pallas kernels: 48.9 us -> 49.8 us  [shards(): pl.pallas_call(functools.partial(kernel, n_blk, n_rep), out_shape=(jax.Sh...]
where the time goes in v3:
time: 56.7 us; the launch traced here: 56.5 us
  Pallas kernels  49.8 us (88%)
  local copies, waits for them, and re-layouts  6.12 us (11%)
  between operations  0.64 us (1%)
    pallas_call x1, Pallas kernels, shards(): pl.pallas_call(functools.partial(kernel, n_blk, n_rep), out_shape=(jax.Sh...  49.8 us
    unnamed x4, local copies, waits for them, and re-layouts  6.12 us

profile of v3, /device:TPU:1, one launch (start us, length us, event | category | flops | bytes accessed | tf_op | source)
XLA Modules:
  0.0 56.5 jit_solution(11462856365674929276)
XLA Ops:
  0.6 49.8 %shard_map.111 = (bf16[12,4,32,128]{3,2,1,0:T(8,128)(2,1)}, f32[2,128,128]{2,1,0:T(8,128)}, f32[2,128,128]{2,1,0:T(8,128)}, f32[2,128]{1,0:T(2,128)}) custom-call(bf16[12,4,32,128]{3,2,1,0:T(8,128)(2,1)} %bitcast.5, bf16[12,24,32,128]{3,2,1,0:T(8,128)(2,1)} %tiles_hbm.1, s32[12,24]{1,0:T(8,128)} %col_hbm.1, s32[4,12]{1,0:T(4,128)} %bitcast.7, ...), custom_call_target="tpu_custom_call" | custom-call | tf_op jit(solution)/shard_map/pallas_call | solution.py:401
  50.4 1.8 %copy.16 = bf16[1536,128]{1,0:T(8,128)(2,1)} copy(bf16[1536,128]{1,0:T(8,128)(2,1)} %bitcast.4) | data formatting | bytes 786432
  52.2 1.6 %copy.17 = f32[2,128,128]{2,1,0:T(8,128)} copy(f32[2,128,128]{2,1,0:T(8,128)} %get-tuple-element.17) | data formatting | bytes 262144
  53.8 1.6 %copy.18 = f32[2,128,128]{2,1,0:T(8,128)} copy(f32[2,128,128]{2,1,0:T(8,128)} %get-tuple-element.18) | data formatting | bytes 262144
  55.3 1.2 %copy.19 = f32[2,128]{1,0:T(2,128)} copy(f32[2,128]{1,0:T(2,128)} %get-tuple-element.19) | data formatting | bytes 2048

commit v4 on v3

--- a/solution.py
+++ b/solution.py
@@ -10,7 +10,7 @@
 MESH = pl.DeviceIdType.MESH
 F32 = jnp.float32
 BF16 = jnp.bfloat16
-HALVES = 2
+HALVES = 3
 
 
 def contract(a, b, a_dim, b_dim):

time: 56.7 us -> 57.2 us (level)
  no operation moved by 1% of the time
where the time goes in v4:
time: 57.2 us; the launch traced here: 57 us
  Pallas kernels  50.2 us (88%)
  local copies, waits for them, and re-layouts  6.12 us (11%)
  between operations  0.64 us (1%)
    pallas_call x1, Pallas kernels, shards(): pl.pallas_call(functools.partial(kernel, n_blk, n_rep), out_shape=(jax.Sh...  50.2 us
    unnamed x4, local copies, waits for them, and re-layouts  6.12 us

profile of v4, /device:TPU:1, one launch (start us, length us, event | category | flops | bytes accessed | tf_op | source)
XLA Modules:
  0.0 57.0 jit_solution(11739852989990966203)
XLA Ops:
  0.6 50.2 %shard_map.111 = (bf16[12,4,32,128]{3,2,1,0:T(8,128)(2,1)}, f32[2,128,128]{2,1,0:T(8,128)}, f32[2,128,128]{2,1,0:T(8,128)}, f32[2,128]{1,0:T(2,128)}) custom-call(bf16[12,4,32,128]{3,2,1,0:T(8,128)(2,1)} %bitcast.5, bf16[12,24,32,128]{3,2,1,0:T(8,128)(2,1)} %tiles_hbm.1, s32[12,24]{1,0:T(8,128)} %col_hbm.1, s32[4,12]{1,0:T(4,128)} %bitcast.7, ...), custom_call_target="tpu_custom_call" | custom-call | tf_op jit(solution)/shard_map/pallas_call | solution.py:401
  50.9 1.8 %copy.16 = bf16[1536,128]{1,0:T(8,128)(2,1)} copy(bf16[1536,128]{1,0:T(8,128)(2,1)} %bitcast.4) | data formatting | bytes 786432
  52.6 1.6 %copy.17 = f32[2,128,128]{2,1,0:T(8,128)} copy(f32[2,128,128]{2,1,0:T(8,128)} %get-tuple-element.17) | data formatting | bytes 262144
  54.2 1.6 %copy.18 = f32[2,128,128]{2,1,0:T(8,128)} copy(f32[2,128,128]{2,1,0:T(8,128)} %get-tuple-element.18) | data formatting | bytes 262144
  55.8 1.2 %copy.19 = f32[2,128]{1,0:T(2,128)} copy(f32[2,128]{1,0:T(2,128)} %get-tuple-element.19) | data formatting | bytes 2048
